TPU v7x, 32 devices: a whole 2x2x4 slice. The times are simulated.
32 devices in a mesh: dp: 2 (over core), fsdp: 16 (over z, y, x).
Axes of the slice: x: 2, y: 2, z: 4, core: 2. Of those that a mesh axis runs over, the one named last changes fastest.
Arguments:
- tokens: bfloat16 [64, 392, 768], P(('dp', 'fsdp')), may hold values from -6 to 6
- positions: int32 [64, 392], P(('dp', 'fsdp')), may hold values from 0 to 1567, as said below
- counts: int32 [64], P(('dp', 'fsdp')), may hold values from 78 to 392, as said below
- cotangent: bfloat16 [64, 392, 768], P(('dp', 'fsdp')), may hold values from -6 to 6
- qkv_weight: float32 [768, 2304], P('fsdp'), may hold values from -0.21875 to 0.21875
- out_weight: float32 [768, 768], P('fsdp'), may hold values from -3.5 to 3.5
- up_weight: float32 [768, 3072], P('fsdp'), may hold values from -0.21875 to 0.21875
- down_weight: float32 [3072, 768], P('fsdp'), may hold values from -0.109375 to 0.109375
- small_params: float32 [768, 12], P('fsdp'), may hold values from -2 to 2
- qkv_momentum: float32 [768, 2304], P('fsdp'), may hold values from -256 to 256
- out_momentum: float32 [768, 768], P('fsdp'), may hold values from -48 to 48
- up_momentum: float32 [768, 3072], P('fsdp'), may hold values from -384 to 384
- down_momentum: float32 [3072, 768], P('fsdp'), may hold values from -384 to 384
- small_momentum: float32 [768, 12], P('fsdp'), may hold values from -512 to 512
- qkv_average: float32 [768, 2304], P('fsdp'), may hold values from -0.21875 to 0.21875
- out_average: float32 [768, 768], P('fsdp'), may hold values from -3.5 to 3.5
- up_average: float32 [768, 3072], P('fsdp'), may hold values from -0.21875 to 0.21875
- down_average: float32 [3072, 768], P('fsdp'), may hold values from -0.109375 to 0.109375
- small_average: float32 [768, 12], P('fsdp'), may hold values from -6 to 6
Outputs:
- block_out: bfloat16 [64, 392, 768], P(('dp', 'fsdp'))
- token_grad: float32 [64, 392, 768], P(('dp', 'fsdp'))
- new_qkv_weight: float32 [768, 2304], P('fsdp')
- new_out_weight: float32 [768, 768], P('fsdp')
- new_up_weight: float32 [768, 3072], P('fsdp')
- new_down_weight: float32 [3072, 768], P('fsdp')
- new_small_params: float32 [768, 12], P('fsdp')
- new_qkv_momentum: float32 [768, 2304], P('fsdp')
- new_out_momentum: float32 [768, 768], P('fsdp')
- new_up_momentum: float32 [768, 3072], P('fsdp')
- new_down_momentum: float32 [3072, 768], P('fsdp')
- new_small_momentum: float32 [768, 12], P('fsdp')
- new_qkv_average: float32 [768, 2304], P('fsdp')
- new_out_average: float32 [768, 768], P('fsdp')
- new_up_average: float32 [768, 3072], P('fsdp')
- new_down_average: float32 [3072, 768], P('fsdp')
- new_small_average: float32 [768, 12], P('fsdp')
- norms: float32 [10], replicated
Inputs may be any that keep to these rules, and one draw needn't show every extreme that they name: `counts`: some clip has exactly 392 visible tubelets and some exactly 78. The 392 positions of a clip are distinct; rows at and after a clip's count are padding.
All inputs are finite; a program needn't handle non-finite values.
Results may differ from a plain program's by a relative error of at most 0.012.
The roundings to bfloat16 on the way count: a program that leaves them out, or rounds other values in their place, can miss the bound.
Values may be sent and summed in bfloat16 or wider, within the bound.
No kernel may reach another device: no remote copies, remote signals or barrier semaphores. Data moves between devices by JAX's collectives and lax.ppermute only.
A program may use at most 256 MiB of HBM per device.

v0:
```python
import math
import jax
import jax.numpy as jnp
from jax import lax
from jax.sharding import PartitionSpec as P

HEAD_DIM = 64
EPS_NORM = 1e-06
MOMENTUM_DECAY = 0.9
WEIGHT_DECAY = 0.0001
TRUST_RATE = 0.2
AVERAGE_DECAY = 0.8


def sinusoid(positions, width):
    half_width = width // 2
    freqs = jnp.exp(jnp.arange(half_width, dtype=jnp.float32) * (-2.0 * math.log(10000.0) / width))
    angles = positions.astype(jnp.float32)[..., None] * freqs
    return jnp.stack([jnp.sin(angles), jnp.cos(angles)], axis=-1).reshape(
        positions.shape + (width,)
    )


def normalize(values):
    center = values - jnp.mean(values, axis=-1, keepdims=True)
    inv_std = lax.rsqrt(jnp.mean(center * center, axis=-1, keepdims=True) + EPS_NORM)
    return (center * inv_std, inv_std)


def norm_back(grad_hat, normed, inv_std):
    first_mean = jnp.mean(grad_hat, axis=-1, keepdims=True)
    second_mean = jnp.mean(grad_hat * normed, axis=-1, keepdims=True)
    return inv_std * (grad_hat - first_mean - normed * second_mean)


def split_small(small_low):
    pieces = [small_low[:, i].astype(jnp.float32) for i in range(8)]
    return (pieces, small_low[:, 8:].astype(jnp.float32).reshape(-1))


def update_group(weight, grad, moment, average, grad_norm, weight_norm):
    effective = grad + WEIGHT_DECAY * weight
    moment_new = MOMENTUM_DECAY * moment + effective
    rate = TRUST_RATE * weight_norm / (grad_norm + WEIGHT_DECAY * weight_norm)
    weight_new = weight - rate * (effective + MOMENTUM_DECAY * moment_new)
    average_new = AVERAGE_DECAY * average + (1.0 - AVERAGE_DECAY) * weight_new
    return (weight_new, moment_new, average_new)


def on_device(
    tokens,
    positions,
    counts,
    cotangent,
    qkv_weight,
    out_weight,
    up_weight,
    down_weight,
    small_params,
    qkv_momentum,
    out_momentum,
    up_momentum,
    down_momentum,
    small_momentum,
    qkv_average,
    out_average,
    up_average,
    down_average,
    small_average,
):
    clip_count, seq_len, width = tokens.shape
    row_count = clip_count * seq_len
    head_count = width // HEAD_DIM
    score_scale = HEAD_DIM ** (-0.5)
    low_qkv = qkv_weight.astype(jnp.bfloat16)
    low_out = out_weight.astype(jnp.bfloat16)
    low_up = up_weight.astype(jnp.bfloat16)
    low_down = down_weight.astype(jnp.bfloat16)
    low_small = small_params.astype(jnp.bfloat16)
    wq_full, wo_full, up_full, down_full, small_full = (
        lax.all_gather(low_qkv, "fsdp", axis=0, tiled=True),
        lax.all_gather(low_out, "fsdp", axis=0, tiled=True),
        lax.all_gather(low_up, "fsdp", axis=0, tiled=True),
        lax.all_gather(low_down, "fsdp", axis=0, tiled=True),
        lax.all_gather(low_small, "fsdp", axis=0, tiled=True),
    )
    pieces, bias_up = split_small(small_full)
    gain_one, shift_one, gain_two, shift_two, bias_query, bias_value, bias_out, bias_down = pieces
    key_ok = jnp.arange(seq_len)[None, :] < counts[:, None]
    row_ok = key_ok.reshape(row_count, 1).astype(jnp.float32)
    embed = (tokens.astype(jnp.float32) + sinusoid(positions, width)).reshape(row_count, width)
    hat_one, inv_one = normalize(embed)
    attn_in = (hat_one * gain_one + shift_one).astype(jnp.bfloat16)
    bias_qkv = jnp.concatenate([bias_query, jnp.zeros((width,), jnp.float32), bias_value])
    qkv_rows = (jnp.dot(attn_in, wq_full, preferred_element_type=jnp.float32) + bias_qkv).astype(
        jnp.bfloat16
    )
    query = qkv_rows[:, :width].reshape(clip_count, seq_len, head_count, HEAD_DIM)
    keys = qkv_rows[:, width : 2 * width].reshape(clip_count, seq_len, head_count, HEAD_DIM)
    values = qkv_rows[:, 2 * width :].reshape(clip_count, seq_len, head_count, HEAD_DIM)

    def attention_scores():
        raw = (
            jnp.einsum("clhe,cmhe->chlm", query, keys, preferred_element_type=jnp.float32)
            * score_scale
        )
        return jnp.where(key_ok[:, None, None, :], raw, -1000000000.0)

    scores = attention_scores()
    row_top = jnp.max(scores, axis=-1, keepdims=True)
    expo = jnp.exp(scores - row_top)
    denominator = jnp.sum(expo, axis=-1, keepdims=True)
    log_total = row_top + jnp.log(denominator)
    attention = expo / denominator
    mixed = jnp.einsum(
        "chlm,cmhe->clhe",
        attention.astype(jnp.bfloat16),
        values,
        preferred_element_type=jnp.float32,
    )
    attn_out = mixed.astype(jnp.bfloat16).reshape(row_count, width)
    resid = embed + jnp.dot(attn_out, wo_full, preferred_element_type=jnp.float32) + bias_out
    hat_two, inv_two = normalize(resid)
    mlp_in = (hat_two * gain_two + shift_two).astype(jnp.bfloat16)
    pre = jnp.dot(mlp_in, up_full, preferred_element_type=jnp.float32) + bias_up
    act = jax.nn.gelu(pre, approximate=False).astype(jnp.bfloat16)
    block_rows = resid + jnp.dot(act, down_full, preferred_element_type=jnp.float32) + bias_down
    block_out = block_rows.astype(jnp.bfloat16).reshape(clip_count, seq_len, width)
    wq_full, wo_full, up_full, down_full, small_full = (
        lax.all_gather(low_qkv, "fsdp", axis=0, tiled=True),
        lax.all_gather(low_out, "fsdp", axis=0, tiled=True),
        lax.all_gather(low_up, "fsdp", axis=0, tiled=True),
        lax.all_gather(low_down, "fsdp", axis=0, tiled=True),
        lax.all_gather(low_small, "fsdp", axis=0, tiled=True),
    )
    pieces, bias_up = split_small(small_full)
    gain_one, shift_one, gain_two, shift_two, bias_query, bias_value, bias_out, bias_down = pieces
    grad_rows = cotangent.astype(jnp.float32).reshape(row_count, width) * row_ok
    grad_down = grad_rows.astype(jnp.bfloat16)
    d_bias_down = jnp.sum(grad_down, axis=0, dtype=jnp.float32)
    d_down_weight = jnp.einsum("rf,rd->fd", act, grad_down, preferred_element_type=jnp.float32)
    d_act = jnp.einsum("rd,fd->rf", grad_down, down_full, preferred_element_type=jnp.float32)
    normal_cdf = 0.5 * (1.0 + lax.erf(pre * 0.7071067811865476))
    normal_pdf = jnp.exp(-0.5 * pre * pre) * 0.3989422804014327
    d_pre = (d_act * (normal_cdf + pre * normal_pdf)).astype(jnp.bfloat16)
    d_bias_up = jnp.sum(d_pre, axis=0, dtype=jnp.float32)
    d_up_weight = jnp.einsum("rd,rf->df", mlp_in, d_pre, preferred_element_type=jnp.float32)
    d_mlp_in = jnp.einsum("rf,df->rd", d_pre, up_full, preferred_element_type=jnp.float32)
    d_gain_two = jnp.sum(d_mlp_in * hat_two, axis=0)
    d_shift_two = jnp.sum(d_mlp_in, axis=0)
    d_resid = grad_rows + norm_back(d_mlp_in * gain_two, hat_two, inv_two)
    grad_proj = d_resid.astype(jnp.bfloat16)
    d_bias_out = jnp.sum(grad_proj, axis=0, dtype=jnp.float32)
    d_out_weight = jnp.einsum("rd,re->de", attn_out, grad_proj, preferred_element_type=jnp.float32)
    d_mixed = jnp.einsum("re,de->rd", grad_proj, wo_full, preferred_element_type=jnp.float32)
    d_mixed = d_mixed.astype(jnp.bfloat16).reshape(clip_count, seq_len, head_count, HEAD_DIM)
    attention = jnp.exp(attention_scores() - log_total)
    d_values = jnp.einsum(
        "chlm,clhe->cmhe",
        attention.astype(jnp.bfloat16),
        d_mixed,
        preferred_element_type=jnp.float32,
    )
    d_attention = jnp.einsum("clhe,cmhe->chlm", d_mixed, values, preferred_element_type=jnp.float32)
    inner = jnp.sum(d_attention * attention, axis=-1, keepdims=True)
    d_scores = (attention * (d_attention - inner)).astype(jnp.bfloat16)
    d_query = (
        jnp.einsum("chlm,cmhe->clhe", d_scores, keys, preferred_element_type=jnp.float32)
        * score_scale
    )
    d_keys = (
        jnp.einsum("chlm,clhe->cmhe", d_scores, query, preferred_element_type=jnp.float32)
        * score_scale
    )
    d_qkv = jnp.concatenate(
        [
            d_query.reshape(row_count, width),
            d_keys.reshape(row_count, width),
            d_values.reshape(row_count, width),
        ],
        axis=1,
    ).astype(jnp.bfloat16)
    d_bias_query = jnp.sum(d_qkv[:, :width], axis=0, dtype=jnp.float32)
    d_bias_value = jnp.sum(d_qkv[:, 2 * width :], axis=0, dtype=jnp.float32)
    d_qkv_weight = jnp.einsum("rd,re->de", attn_in, d_qkv, preferred_element_type=jnp.float32)
    d_attn_in = jnp.einsum("re,de->rd", d_qkv, wq_full, preferred_element_type=jnp.float32)
    d_gain_one = jnp.sum(d_attn_in * hat_one, axis=0)
    d_shift_one = jnp.sum(d_attn_in, axis=0)
    token_grad = (d_resid + norm_back(d_attn_in * gain_one, hat_one, inv_one)).reshape(
        clip_count, seq_len, width
    )
    d_columns = jnp.stack(
        [
            d_gain_one,
            d_shift_one,
            d_gain_two,
            d_shift_two,
            d_bias_query,
            d_bias_value,
            d_bias_out,
            d_bias_down,
        ],
        axis=1,
    )
    d_small = jnp.concatenate([d_columns, d_bias_up.reshape(width, -1)], axis=1)
    shard_qkv, shard_out, shard_up, shard_down, shard_small = (
        lax.psum_scatter(d_qkv_weight, "fsdp", scatter_dimension=0, tiled=True),
        lax.psum_scatter(d_out_weight, "fsdp", scatter_dimension=0, tiled=True),
        lax.psum_scatter(d_up_weight, "fsdp", scatter_dimension=0, tiled=True),
        lax.psum_scatter(d_down_weight, "fsdp", scatter_dimension=0, tiled=True),
        lax.psum_scatter(d_small, "fsdp", scatter_dimension=0, tiled=True),
    )
    grads = (
        lax.psum(shard_qkv.astype(jnp.bfloat16), "dp").astype(jnp.float32),
        lax.psum(shard_out.astype(jnp.bfloat16), "dp").astype(jnp.float32),
        lax.psum(shard_up.astype(jnp.bfloat16), "dp").astype(jnp.float32),
        lax.psum(shard_down.astype(jnp.bfloat16), "dp").astype(jnp.float32),
        lax.psum(shard_small.astype(jnp.bfloat16), "dp").astype(jnp.float32),
    )
    masters = (qkv_weight, out_weight, up_weight, down_weight, small_params)
    moments = (qkv_momentum, out_momentum, up_momentum, down_momentum, small_momentum)
    averages = (qkv_average, out_average, up_average, down_average, small_average)
    squares = jnp.stack(
        [jnp.sum(grad * grad) for grad in grads] + [jnp.sum(weight * weight) for weight in masters]
    )
    totals = lax.psum(squares, "fsdp")
    norms = jnp.sqrt(totals)
    results = [
        update_group(masters[i], grads[i], moments[i], averages[i], norms[i], norms[5 + i])
        for i in range(5)
    ]
    return (
        block_out,
        token_grad,
        results[0][0],
        results[1][0],
        results[2][0],
        results[3][0],
        results[4][0],
        results[0][1],
        results[1][1],
        results[2][1],
        results[3][1],
        results[4][1],
        results[0][2],
        results[1][2],
        results[2][2],
        results[3][2],
        results[4][2],
        norms,
    )


def solution(mesh):
    in_specs = (
        P(("dp", "fsdp"), None, None),
        P(("dp", "fsdp"), None),
        P(("dp", "fsdp")),
        P(("dp", "fsdp"), None, None),
        P("fsdp", None),
        P("fsdp", None),
        P("fsdp", None),
        P("fsdp", None),
        P("fsdp", None),
        P("fsdp", None),
        P("fsdp", None),
        P("fsdp", None),
        P("fsdp", None),
        P("fsdp", None),
        P("fsdp", None),
        P("fsdp", None),
        P("fsdp", None),
        P("fsdp", None),
        P("fsdp", None),
    )
    out_specs = (
        P(("dp", "fsdp"), None, None),
        P(("dp", "fsdp"), None, None),
        P("fsdp", None),
        P("fsdp", None),
        P("fsdp", None),
        P("fsdp", None),
        P("fsdp", None),
        P("fsdp", None),
        P("fsdp", None),
        P("fsdp", None),
        P("fsdp", None),
        P("fsdp", None),
        P("fsdp", None),
        P("fsdp", None),
        P("fsdp", None),
        P("fsdp", None),
        P("fsdp", None),
        P(),
    )
    return jax.shard_map(
        on_device, mesh=mesh, in_specs=in_specs, out_specs=out_specs, check_vma=False
    )
```

profile of v0, /device:TPU:0, one launch (start us, length us, event | category | flops | bytes accessed | tf_op | source)
XLA Modules:
  0.0 1200.0 jit_solution(15293713448543002065)
XLA Ops:
  18.3 42.9 %all-gather = bf16[16,48,12]{1,2,0:T(8,128)(2,1)S(1)} all-gather(bf16[1,48,12]{1,2,0:T(8,128)(2,1)S(1)} %get-tuple-element.105), channel_id=1, replica_groups=mesh['dp'=2,'fsdp'=16] {'fsdp'}, dimensions={0}, use_global_device_ids=true | all-gather | bytes 19584 | tf_op jit(solution)/shard_map/all_gather | solution.py:85
  62.1 3.1 copy.169
  65.1 4.2 multiply_sine_fusion
  69.5 3.5 copy.170
  73.1 4.6 fusion.59
  79.5 3.5 copy.171
  88.2 5.7 add_convert_fusion
  95.2 3.0 reshape.315
  98.2 3.9 copy.177
  102.2 3.1 reshape.314
  105.2 3.9 copy.176
  109.2 5.0 reshape.313
  114.2 4.8 copy.178
  119.0 9.3 fusion.22
  128.3 11.1 fusion
  139.4 9.1 fusion.32
  152.3 3.8 bitcast_add_fusion.1
  156.8 69.6 %all-gather.10.cloned.1.call-done = bf16[768,3072]{1,0:T(8,128)(2,1)} async-done(((bf16[48,3072]{1,0:T(8,128)(2,1)}), bf16[768,3072]{1,0:T(8,128)(2,1)}) %all-gather.10.cloned.1.call-update) | async-done | bytes 4718608 | tf_op jit(solution)/shard_map/all_gather | solution.py:83
  226.4 27.8 %fusion.4 = (bf16[784,3072]{1,0:T(8,128)(2,1)}, f32[784,3072]{1,0:T(8,128)}) fusion(f32[3072]{0:T(1024)S(1)} %reshape.306, bf16[768,3072]{1,0:T(8,128)(2,1)} %all-gather.10.cloned.1.call-done, f32[768]{0:T(1024)S(1)} %get-tuple-element.63, f32[768]{0:T(1024)S(1)} %get-tuple-element.64, f32[784]{0:T(1024)S(1)} %add_rsqrt_fusion, ...), kind=kOutput, calls=%fused_computation.12 | convolution fusion | flops 3861946368 | bytes 21605504 | tf_op jit(solution)/shard_map/dot_general | solution.py:125
  254.3 54.5 %all-gather.12.cloned.1.call-done = bf16[3072,768]{1,0:T(8,128)(2,1)} async-done(((bf16[192,768]{1,0:T(8,128)(2,1)}), bf16[3072,768]{1,0:T(8,128)(2,1)}) %all-gather.12.cloned.1.call-update) | async-done | bytes 4718608 | tf_op jit(solution)/shard_map/all_gather | solution.py:84
  308.8 10.0 convert_reduce_fusion
  318.8 4.5 multiply_reduce_fusion.2
  326.6 2.8 fusion.51
  329.5 4.2 convolution_convert_fusion
  333.6 4.8 reshape.316
  338.4 4.9 copy.183
  343.2 15.5 %multiply_reduce_fusion = (f32[2,12,392]{2,1,0:T(8,128)S(1)}, f32[2,12,392,392]{2,3,1,0:T(8,128)}) fusion(f32[2,12,392]{2,1,0:T(8,128)S(1)} %log_add_fusion, f32[2,12,392,392]{2,3,1,0:T(8,128)} %get-tuple-element.121, pred[2,392]{1,0:T(4,128)(4,1)S(1)} %get-tuple-element.119, bf16[2,392,12,64]{1,3,2,0:T(8,128)(2,1)} %copy.183, ...), kind=kOutput, calls=%fused_computation.1 | convolution fusion | flops 490486080 | bytes 31987984 | tf_op jit(solution)/shard_map/clhe,cmhe->chlm/dot_general | solution.py:164
  358.7 9.1 fusion.29
  370.6 4.7 reshape.296
  375.3 14.8 %multiply_convert_fusion = bf16[2,12,392,392]{2,3,1,0:T(8,128)(2,1)S(1)} fusion(f32[2,12,392,392]{2,3,1,0:T(8,128)} %get-tuple-element.124, f32[2,12,392]{2,1,0:T(8,128)S(1)} %get-tuple-element.123, f32[2,12,392]{2,1,0:T(8,128)S(1)} %log_add_fusion, f32[2,12,392,392]{2,3,1,0:T(8,128)} %get-tuple-element.121, pred[2,392]{1,0:T(4,128)(4,1)S(1)} %get-tuple-element.119), kind=kLoop, calls=%fused_computation | loop fusion | flops 22127616 | bytes 36955408 | tf_op jit(solution)/shard_map/convert_element_type | solution.py:166
  393.8 2.8 copy.187
  396.6 4.8 reshape.294
  401.3 7.2 fusion.34
  408.5 2.8 copy.190
  411.3 5.0 reshape.295
  420.7 6.0 fusion.38
  426.8 10.3 fusion.39
  437.1 9.5 fusion.62
  452.8 8.9 multiply_reduce_fusion.3
  464.4 148.5 %reduce-scatter.8.cloned.1.call-done = f32[48,2304]{1,0:T(8,128)} async-done(((f32[768,2304]{1,0:T(8,128)}), f32[48,2304]{1,0:T(8,128)}) %reduce-scatter.8.cloned.1.call-update) | async-done | bytes 442384 | tf_op jit(solution)/shard_map/reduce_scatter | solution.py:207
  614.6 174.0 %reduce-scatter.12.cloned.1.call-done = f32[48,3072]{1,0:T(8,128)} async-done(((f32[768,3072]{1,0:T(8,128)}), f32[48,3072]{1,0:T(8,128)}) %reduce-scatter.12.cloned.1.call-update) | async-done | bytes 589840 | tf_op jit(solution)/shard_map/reduce_scatter | solution.py:209
  790.4 173.9 %reduce-scatter.14.cloned.1.call-done = f32[192,768]{1,0:T(8,128)} async-done(((f32[3072,768]{1,0:T(8,128)}), f32[192,768]{1,0:T(8,128)}) %reduce-scatter.14.cloned.1.call-update) | async-done | bytes 589840 | tf_op jit(solution)/shard_map/reduce_scatter | solution.py:210
  966.2 8.7 add_convert_fusion.1
  974.9 115.7 %reduce-scatter.16.cloned.1.call-done = f32[48,12]{1,0:T(8,128)} async-done(((f32[768,12]{1,0:T(8,128)}), f32[48,12]{1,0:T(8,128)}) %reduce-scatter.16.cloned.1.call-update) | async-done | bytes 2320
  1094.5 18.2 %all-reduce.3.cloned.1.call-done = (bf16[48,2304]{1,0:T(8,128)(2,1)}, bf16[48,768]{1,0:T(8,128)(2,1)}, bf16[48,3072]{1,0:T(8,128)(2,1)}, bf16[192,768]{1,0:T(8,128)(2,1)}) async-done(((bf16[48,2304]{1,0:T(8,128)(2,1)}, bf16[48,768]{1,0:T(8,128)(2,1)}, bf16[48,3072]{1,0:T(8,128)(2,1)}, bf16[192,768]{1,0:T(8,128)(2,1)}), (bf16[48,2304]{1,0:T(8,128)(2,1)}, bf16[48,768]{1,0:T(8,128)(2,1)}, ...) | async-done | bytes 884752 | tf_op jit(solution)/shard_map/psum | solution.py:214
  1119.3 6.5 stack.81
  1125.9 4.6 multiply_add_fusion
  1130.6 42.6 %psum.47 = f32[10]{0:T(128)} all-reduce(f32[10]{0:T(128)S(1)} %stack.81), channel_id=1, replica_groups=mesh['dp'=2,'fsdp'=16] {'fsdp'}, use_global_device_ids=true, to_apply=%region_40.41 | all-reduce | flops 10 | bytes 80 | tf_op jit(solution)/shard_map/psum | solution.py:226
  (196 shorter events, 72.9 us)
Async XLA Ops:
  7.2 10.5 copy-start.39
  7.2 54.8 %copy-start.46 = (s32[2,392]{1,0:T(2,128)S(1)}, s32[2,392]{1,0:T(2,128)}, u32[]{:S(2)}) copy-start(s32[2,392]{1,0:T(2,128)} %param.20) | copy-start | bytes 9412
  7.2 54.8 %copy-start.17 = (bf16[2,392,768]{2,1,0:T(8,128)(2,1)S(1)}, bf16[2,392,768]{2,1,0:T(8,128)(2,1)}, u32[]{:S(2)}) copy-start(bf16[2,392,768]{2,1,0:T(8,128)(2,1)} %param.19) | copy-start | bytes 3612676
  7.2 81.0 %all-gather.6.cloned.1.call-start = ((), (), s32[]{:S(2)}) async-start(), calls=%async_computation.5 | async-start | bytes 3760128 | tf_op jit(solution)/shard_map/all_gather | solution.py:81
  9.8 142.4 %all-gather.8.cloned.1.call-start = ((), (), s32[]{:S(2)}) async-start(), calls=%async_computation.6 | async-start | bytes 1253376 | tf_op jit(solution)/shard_map/all_gather | solution.py:82
  12.2 214.3 %all-gather.10.cloned.1.call-start = ((), (), s32[]{:S(2)}) async-start(), calls=%async_computation.7 | async-start | bytes 5013504 | tf_op jit(solution)/shard_map/all_gather | solution.py:83
  14.9 293.9 %all-gather.12.cloned.1.call-start = ((), (), s32[]{:S(2)}) async-start(), calls=%async_computation.8 | async-start | bytes 5013504 | tf_op jit(solution)/shard_map/all_gather | solution.py:84
  17.7 445.1 %reduce-scatter.10.cloned.1.call-start = ((), (), s32[]{:S(2)}) async-start(), calls=%async_computation.10 | async-start | bytes 2506752 | tf_op jit(solution)/shard_map/reduce_scatter | solution.py:208
  62.0 26.2 %copy-start.41 = (f32[768]{0:T(1024)}, f32[768]{0:T(1024)S(1)}, u32[]{:S(2)}) copy-start(f32[768]{0:T(1024)S(1)} %get-tuple-element.69) | copy-start | bytes 9220
  62.0 26.2 %copy-start.44 = (f32[768]{0:T(1024)}, f32[768]{0:T(1024)S(1)}, u32[]{:S(2)}) copy-start(f32[768]{0:T(1024)S(1)} %get-tuple-element.68) | copy-start | bytes 9220
  77.7 8.7 copy-start.33
  79.5 3.5 copy-start.47
  83.2 4.9 copy-start.31
  83.8 4.3 copy-start.35
  102.1 16.8 %copy-start.2 = (bf16[2,392,12,64]{1,3,2,0:T(8,128)(2,1)}, bf16[2,392,12,64]{1,3,2,0:T(8,128)(2,1)S(1)}, u32[]{:S(2)}) copy-start(bf16[2,392,12,64]{1,3,2,0:T(8,128)(2,1)S(1)} %copy.177) | copy-start | bytes 3612676
  109.2 9.8 copy-start.4
  128.3 11.1 copy-start.8
  308.8 10.0 copy-start.48
  318.8 4.6 copy-start.11
  318.8 4.6 copy-start.6
  318.8 4.6 copy-start.32
  329.4 283.5 %reduce-scatter.8.cloned.1.call-start = ((), (), s32[]{:S(2)}) async-start(), calls=%async_computation.9 | async-start | bytes 7520256 | tf_op jit(solution)/shard_map/reduce_scatter | solution.py:207
  343.2 15.5 %copy-start.9 = (bf16[2,392,12,64]{1,3,2,0:T(8,128)(2,1)S(1)}, bf16[2,392,12,64]{1,3,2,0:T(8,128)(2,1)}, u32[]{:S(2)}) copy-start(bf16[2,392,12,64]{1,3,2,0:T(8,128)(2,1)} %copy.183) | copy-start | bytes 3612676
  375.3 14.8 %copy-start.3 = (bf16[2,392,12,64]{1,3,2,0:T(8,128)(2,1)S(1)}, bf16[2,392,12,64]{1,3,2,0:T(8,128)(2,1)}, u32[]{:S(2)}) copy-start(bf16[2,392,12,64]{1,3,2,0:T(8,128)(2,1)} %copy-done.2) | copy-start | bytes 3612676
  390.1 3.7 copy-start
  426.7 361.9 %reduce-scatter.12.cloned.1.call-start = ((), (), s32[]{:S(2)}) async-start(), calls=%async_computation.11 | async-start | bytes 10027008 | tf_op jit(solution)/shard_map/reduce_scatter | solution.py:209
  437.1 527.2 %reduce-scatter.14.cloned.1.call-start = ((), (), s32[]{:S(2)}) async-start(), calls=%async_computation.12 | async-start | bytes 10027008 | tf_op jit(solution)/shard_map/reduce_scatter | solution.py:210
  446.6 643.9 %reduce-scatter.16.cloned.1.call-start = ((), (), s32[]{:S(2)}) async-start(), calls=%async_computation.13 | async-start | bytes 417792
  461.7 504.4 %copy-start.43 = (f32[768]{0:T(1024)S(1)}, f32[768]{0:T(1024)}, u32[]{:S(2)}) copy-start(f32[768]{0:T(1024)} %get-tuple-element.62) | copy-start | bytes 9220
  462.7 649.9 %all-reduce.3.cloned.1.call-start = ((), (), s32[]{:S(2)}) async-start(), calls=%async_computation.14 | async-start | bytes 1769472 | tf_op jit(solution)/shard_map/psum | solution.py:214
  966.1 159.7 %copy-start.34 = (f32[784]{0:T(1024)S(1)}, f32[784]{0:T(1024)}, u32[]{:S(2)}) copy-start(f32[784]{0:T(1024)} %copy-done.33) | copy-start | bytes 9412
  966.1 159.7 %copy-start.36 = (f32[784]{0:T(1024)S(1)}, f32[784]{0:T(1024)}, u32[]{:S(2)}) copy-start(f32[784]{0:T(1024)} %copy-done.35) | copy-start | bytes 9412
  1125.8 58.6 %copy-start.40 = (f32[48,12]{0,1:T(8,128)S(1)}, f32[48,12]{0,1:T(8,128)}, u32[]{:S(2)}) copy-start(f32[48,12]{0,1:T(8,128)} %param.27) | copy-start | bytes 6916
  1125.8 59.9 %copy-start.21 = (f32[48,768]{1,0:T(8,128)S(1)}, f32[48,768]{1,0:T(8,128)}, u32[]{:S(2)}) copy-start(f32[48,768]{1,0:T(8,128)} %param.24) | copy-start | bytes 442372
  1125.8 59.9 %copy-start.28 = (bf16[48,768]{1,0:T(8,128)(2,1)S(1)}, bf16[48,768]{1,0:T(8,128)(2,1)}, u32[]{:S(2)}) copy-start(bf16[48,768]{1,0:T(8,128)(2,1)} %get-tuple-element.71) | copy-start | bytes 221188
  1125.9 59.9 %copy-start.29 = (f32[48,768]{1,0:T(8,128)S(1)}, f32[48,768]{1,0:T(8,128)}, u32[]{:S(2)}) copy-start(f32[48,768]{1,0:T(8,128)} %param.34) | copy-start | bytes 442372
  1125.9 61.6 %copy-start.15 = (f32[48,2304]{1,0:T(8,128)S(1)}, f32[48,2304]{1,0:T(8,128)}, u32[]{:S(2)}) copy-start(f32[48,2304]{1,0:T(8,128)} %param.23) | copy-start | bytes 1327108
  1125.9 61.6 %copy-start.20 = (bf16[48,2304]{1,0:T(8,128)(2,1)S(1)}, bf16[48,2304]{1,0:T(8,128)(2,1)}, u32[]{:S(2)}) copy-start(bf16[48,2304]{1,0:T(8,128)(2,1)} %get-tuple-element.70) | copy-start | bytes 663556
  1125.9 61.6 %copy-start.27 = (f32[48,2304]{1,0:T(8,128)S(1)}, f32[48,2304]{1,0:T(8,128)}, u32[]{:S(2)}) copy-start(f32[48,2304]{1,0:T(8,128)} %param.33) | copy-start | bytes 1327108
  1130.5 59.3 %copy-start.13 = (f32[192,768]{1,0:T(8,128)S(1)}, f32[192,768]{1,0:T(8,128)}, u32[]{:S(2)}) copy-start(f32[192,768]{1,0:T(8,128)} %param.26) | copy-start | bytes 1769476
  1130.5 59.3 %copy-start.19 = (bf16[192,768]{1,0:T(8,128)(2,1)S(1)}, bf16[192,768]{1,0:T(8,128)(2,1)}, u32[]{:S(2)}) copy-start(bf16[192,768]{1,0:T(8,128)(2,1)} %get-tuple-element.73) | copy-start | bytes 884740
  1130.5 59.3 %copy-start.22 = (f32[192,768]{1,0:T(8,128)S(1)}, f32[192,768]{1,0:T(8,128)}, u32[]{:S(2)}) copy-start(f32[192,768]{1,0:T(8,128)} %param.36) | copy-start | bytes 1769476
  1130.6 59.3 %copy-start.23 = (f32[192,768]{1,0:T(8,128)S(1)}, f32[192,768]{1,0:T(8,128)}, u32[]{:S(2)}) copy-start(f32[192,768]{1,0:T(8,128)} %param.31) | copy-start | bytes 1769476
  1173.9 17.4 %copy-start.30 = (f32[10]{0:T(128)}, f32[10]{0:T(128)S(1)}, u32[]{:S(2)}) copy-start(f32[10]{0:T(128)S(1)} %sqrt.3) | copy-start | bytes 124
  1187.5 3.8 copy-start.14
  1187.5 3.8 copy-start.18
  1187.5 3.8 copy-start.24
  1187.5 3.8 copy-start.25
  (11 other events, 23.1 us)
Sparse Core Ops, SparseCore 0:
  11.4 74.0 all-gather.5
  88.9 54.6 all-gather.7
  147.0 79.3 all-gather.9
  229.6 79.0 all-gather.11
  329.5 126.9 reduce-scatter.9
  462.5 150.3 reduce-scatter.7
  619.5 169.0 reduce-scatter.11
  794.3 169.9 reduce-scatter.13
  970.2 120.3 reduce-scatter.15
  1094.1 18.4 all-reduce.2
where the time goes:
time: 1210 us; the launch traced here: 1200 us
  waiting for transfers between devices  755 us (62%)
  matrix products  154 us (13%)
  local copies, waits for them, and re-layouts  90.5 us (7%)
  blocking collectives  88 us (7%)
  other arithmetic  86.6 us (7%)
  between operations  25.3 us (2%)
    reduce_scatter x1, waiting for transfers between devices, on_device(): lax.psum_scatter(d_up_weight, 'fsdp', scatter_dimension=0, tiled=True)  174 us
    reduce_scatter x1, waiting for transfers between devices, on_device(): lax.psum_scatter(d_down_weight, 'fsdp', scatter_dimension=0, tiled=True)  174 us
    reduce_scatter x1, waiting for transfers between devices, on_device(): lax.psum_scatter(d_qkv_weight, 'fsdp', scatter_dimension=0, tiled=True)  149 us
    unnamed x11, waiting for transfers between devices  116 us
    all_gather x1, waiting for transfers between devices, on_device(): lax.all_gather(low_up, 'fsdp', axis=0, tiled=True)  69.6 us
    all_gather x1, waiting for transfers between devices, on_device(): lax.all_gather(low_down, 'fsdp', axis=0, tiled=True)  54.5 us
    all_gather x1, blocking collectives, on_device(): lax.all_gather(low_small, 'fsdp', axis=0, tiled=True)  42.9 us
    psum x1, blocking collectives, on_device(): totals = lax.psum(squares, 'fsdp')  42.6 us
  transfers between devices with their start and end apart: 10, of which 7 were waited for; matrix products, arithmetic and copies ran while one was open for 23% of the time, Pallas kernels for 0%

commit v1 on v0

--- a/solution.py
+++ b/solution.py
@@ -10,6 +10,19 @@
 WEIGHT_DECAY = 0.0001
 TRUST_RATE = 0.2
 AVERAGE_DECAY = 0.8
+
+
+def collect(shard, axis, dim):
+    size, index, width = (lax.axis_size(axis), lax.axis_index(axis), shard.shape[dim])
+    upward = [(i, (i + 1) % size) for i in range(size)]
+    out = jnp.zeros((*shard.shape[:dim], size * width, *shard.shape[dim + 1 :]), shard.dtype)
+    held = shard
+    for step in range(size):
+        source = (index - step) % size
+        out = lax.dynamic_update_slice_in_dim(out, held, source * width, axis=dim)
+        if step < size - 1:
+            held = lax.ppermute(held, axis, upward)
+    return out
 
 
 def sinusoid(positions, width):
@@ -81,7 +94,7 @@
         lax.all_gather(low_qkv, "fsdp", axis=0, tiled=True),
         lax.all_gather(low_out, "fsdp", axis=0, tiled=True),
         lax.all_gather(low_up, "fsdp", axis=0, tiled=True),
-        lax.all_gather(low_down, "fsdp", axis=0, tiled=True),
+        collect(low_down, "fsdp", 0),
         lax.all_gather(low_small, "fsdp", axis=0, tiled=True),
     )
     pieces, bias_up = split_small(small_full)

time: 1210 us -> 1260 us (1.041)
  local copies, waits for them, and re-layouts: 90.5 us -> 116 us
  waiting for transfers between devices: 755 us -> 779 us
    ppermute x0 -> x15, waiting for transfers between devices: none -> 180 us  [collect(): held = lax.ppermute(held, axis, upward)]
    reduce_scatter x1, waiting for transfers between devices: 149 us -> 0.01 us  [on_device(): lax.psum_scatter(d_qkv_weight, 'fsdp', scatter_dimension=0, tiled=True)]
    dynamic_update_slice x0 -> x15, local copies, waits for them, and re-layouts: none -> 18.9 us  [collect(): out = lax.dynamic_update_slice_in_dim(out, held, source * width, axis=dim)]
  transfers between devices with their start and end apart: 10 -> 25, of which waited for: 7 -> 21; matrix products, arithmetic and copies ran while one was open for 23% -> 24% of each run, Pallas kernels for 0% -> 0%
where the time goes in v1:
time: 1260 us; the launch traced here: 1250 us
  waiting for transfers between devices  779 us (62%)
  matrix products  154 us (12%)
  local copies, waits for them, and re-layouts  116 us (9%)
  blocking collectives  87.6 us (7%)
  other arithmetic  83.7 us (7%)
  between operations  25.4 us (2%)
    ppermute x15, waiting for transfers between devices, collect(): held = lax.ppermute(held, axis, upward)  180 us
    reduce_scatter x1, waiting for transfers between devices, on_device(): lax.psum_scatter(d_down_weight, 'fsdp', scatter_dimension=0, tiled=True)  174 us
    reduce_scatter x1, waiting for transfers between devices, on_device(): lax.psum_scatter(d_up_weight, 'fsdp', scatter_dimension=0, tiled=True)  167 us
    unnamed x11, waiting for transfers between devices  116 us
    all_gather x1, waiting for transfers between devices, on_device(): lax.all_gather(low_up, 'fsdp', axis=0, tiled=True)  69.2 us
    all_gather x1, waiting for transfers between devices, on_device(): lax.all_gather(low_down, 'fsdp', axis=0, tiled=True)  54.5 us
    all_gather x1, blocking collectives, on_device(): lax.all_gather(low_small, 'fsdp', axis=0, tiled=True)  43 us
    psum x1, blocking collectives, on_device(): totals = lax.psum(squares, 'fsdp')  42.1 us
  transfers between devices with their start and end apart: 25, of which 21 were waited for; matrix products, arithmetic and copies ran while one was open for 24% of the time, Pallas kernels for 0%

profile of v1, /device:TPU:0, one launch (start us, length us, event | category | flops | bytes accessed | tf_op | source)
XLA Modules:
  0.0 1248.2 jit_solution(12702171634024828418)
XLA Ops:
  18.9 43.0 %all-gather = bf16[16,48,12]{1,2,0:T(8,128)(2,1)S(1)} all-gather(bf16[1,48,12]{1,2,0:T(8,128)(2,1)S(1)} %get-tuple-element.105), channel_id=1, replica_groups=mesh['dp'=2,'fsdp'=16] {'fsdp'}, dimensions={0}, use_global_device_ids=true | all-gather | bytes 19584 | tf_op jit(solution)/shard_map/all_gather | solution.py:98
  73.7 4.6 fusion.59
  88.8 5.7 add_convert_fusion
  109.8 5.0 reshape.313
  114.7 4.8 copy.178
  119.5 9.3 fusion.22
  128.9 10.9 fusion
  139.8 9.1 fusion.32
  157.3 69.2 %all-gather.10.cloned.1.call-done = bf16[768,3072]{1,0:T(8,128)(2,1)} async-done(((bf16[48,3072]{1,0:T(8,128)(2,1)}), bf16[768,3072]{1,0:T(8,128)(2,1)}) %all-gather.10.cloned.1.call-update) | async-done | bytes 4718608 | tf_op jit(solution)/shard_map/all_gather | solution.py:96
  226.4 27.8 %fusion.4 = (bf16[784,3072]{1,0:T(8,128)(2,1)}, f32[784,3072]{1,0:T(8,128)}) fusion(f32[3072]{0:T(1024)S(1)} %reshape.306, bf16[768,3072]{1,0:T(8,128)(2,1)} %all-gather.10.cloned.1.call-done, f32[768]{0:T(1024)S(1)} %get-tuple-element.63, f32[768]{0:T(1024)S(1)} %get-tuple-element.64, f32[784]{0:T(1024)S(1)} %add_rsqrt_fusion, ...), kind=kOutput, calls=%fused_computation.12 | convolution fusion | flops 3861946368 | bytes 21605504 | tf_op jit(solution)/shard_map/dot_general | solution.py:138
  254.3 54.5 %all-gather.12.cloned.1.call-done = bf16[3072,768]{1,0:T(8,128)(2,1)} async-done(((bf16[192,768]{1,0:T(8,128)(2,1)}), bf16[3072,768]{1,0:T(8,128)(2,1)}) %all-gather.12.cloned.1.call-update) | async-done | bytes 4718608 | tf_op jit(solution)/shard_map/all_gather | solution.py:146
  308.8 10.0 convert_reduce_fusion
  333.6 4.8 reshape.316
  338.4 4.9 copy.183
  343.3 15.5 %multiply_reduce_fusion = (f32[2,12,392]{2,1,0:T(8,128)S(1)}, f32[2,12,392,392]{2,3,1,0:T(8,128)}) fusion(f32[2,12,392]{2,1,0:T(8,128)S(1)} %log_add_fusion, f32[2,12,392,392]{2,3,1,0:T(8,128)} %get-tuple-element.121, pred[2,392]{1,0:T(4,128)(4,1)S(1)} %get-tuple-element.119, bf16[2,392,12,64]{1,3,2,0:T(8,128)(2,1)} %copy.183, ...), kind=kOutput, calls=%fused_computation.1 | convolution fusion | flops 490486080 | bytes 31987984 | tf_op jit(solution)/shard_map/clhe,cmhe->chlm/dot_general | solution.py:177
  358.7 9.1 fusion.29
  370.6 4.7 reshape.296
  375.4 14.8 %multiply_convert_fusion = bf16[2,12,392,392]{2,3,1,0:T(8,128)(2,1)S(1)} fusion(f32[2,12,392,392]{2,3,1,0:T(8,128)} %get-tuple-element.124, f32[2,12,392]{2,1,0:T(8,128)S(1)} %get-tuple-element.123, f32[2,12,392]{2,1,0:T(8,128)S(1)} %log_add_fusion, f32[2,12,392,392]{2,3,1,0:T(8,128)} %get-tuple-element.121, pred[2,392]{1,0:T(4,128)(4,1)S(1)} %get-tuple-element.119), kind=kLoop, calls=%fused_computation | loop fusion | flops 22127616 | bytes 36955408 | tf_op jit(solution)/shard_map/convert_element_type | solution.py:179
  396.6 4.8 reshape.294
  401.4 7.2 fusion.34
  411.3 5.0 reshape.295
  421.8 6.0 fusion.38
  427.9 10.3 fusion.39
  438.2 9.5 fusion.62
  450.1 11.2 collective-permute-done
  462.1 11.1 collective-permute-done.1
  473.2 18.5 %collective-permute-done.2 = bf16[192,768]{1,0:T(8,128)(2,1)S(1)} collective-permute-done((bf16[192,768]{1,0:T(8,128)(2,1)S(1)}, bf16[192,768]{1,0:T(8,128)(2,1)S(1)}, u32[]{:S(2)}, u32[]{:S(2)}) %collective-permute-start.2) | collective-permute-done | bytes 294944 | tf_op jit(solution)/shard_map/ppermute | solution.py:24
  491.7 18.3 %collective-permute-done.3 = bf16[192,768]{1,0:T(8,128)(2,1)S(1)} collective-permute-done((bf16[192,768]{1,0:T(8,128)(2,1)S(1)}, bf16[192,768]{1,0:T(8,128)(2,1)S(1)}, u32[]{:S(2)}, u32[]{:S(2)}) %collective-permute-start.3) | collective-permute-done | bytes 294944 | tf_op jit(solution)/shard_map/ppermute | solution.py:24
  510.8 16.8 %collective-permute-done.4 = bf16[192,768]{1,0:T(8,128)(2,1)S(1)} collective-permute-done((bf16[192,768]{1,0:T(8,128)(2,1)S(1)}, bf16[192,768]{1,0:T(8,128)(2,1)S(1)}, u32[]{:S(2)}, u32[]{:S(2)}) %collective-permute-start.4) | collective-permute-done | bytes 294944 | tf_op jit(solution)/shard_map/ppermute | solution.py:24
  528.3 10.9 collective-permute-done.5
  539.9 10.5 collective-permute-done.6
  550.4 10.5 collective-permute-done.7
  560.9 10.6 collective-permute-done.8
  573.8 10.5 collective-permute-done.9
  588.6 9.3 collective-permute-done.10
  602.0 8.8 collective-permute-done.11
  614.9 15.0 %collective-permute-done.12 = bf16[192,768]{1,0:T(8,128)(2,1)S(1)} collective-permute-done((bf16[192,768]{1,0:T(8,128)(2,1)S(1)}, bf16[192,768]{1,0:T(8,128)(2,1)S(1)}, u32[]{:S(2)}, u32[]{:S(2)}) %collective-permute-start.12) | collective-permute-done | bytes 294944 | tf_op jit(solution)/shard_map/ppermute | solution.py:24
  634.1 8.1 collective-permute-done.13
  644.7 9.7 collective-permute-done.14
  659.0 8.9 multiply_reduce_fusion.3
  672.4 167.5 %reduce-scatter.12.cloned.1.call-done = f32[48,3072]{1,0:T(8,128)} async-done(((f32[768,3072]{1,0:T(8,128)}), f32[48,3072]{1,0:T(8,128)}) %reduce-scatter.12.cloned.1.call-update) | async-done | bytes 589840 | tf_op jit(solution)/shard_map/reduce_scatter | solution.py:222
  841.7 173.7 %reduce-scatter.14.cloned.1.call-done = f32[192,768]{1,0:T(8,128)} async-done(((f32[3072,768]{1,0:T(8,128)}), f32[192,768]{1,0:T(8,128)}) %reduce-scatter.14.cloned.1.call-update) | async-done | bytes 589840 | tf_op jit(solution)/shard_map/reduce_scatter | solution.py:223
  1017.2 8.7 add_convert_fusion.1
  1025.9 115.7 %reduce-scatter.16.cloned.1.call-done = f32[48,12]{1,0:T(8,128)} async-done(((f32[768,12]{1,0:T(8,128)}), f32[48,12]{1,0:T(8,128)}) %reduce-scatter.16.cloned.1.call-update) | async-done | bytes 2320
  1145.5 18.2 %all-reduce.3.cloned.1.call-done = (bf16[48,2304]{1,0:T(8,128)(2,1)}, bf16[48,768]{1,0:T(8,128)(2,1)}, bf16[48,3072]{1,0:T(8,128)(2,1)}, bf16[192,768]{1,0:T(8,128)(2,1)}) async-done(((bf16[48,2304]{1,0:T(8,128)(2,1)}, bf16[48,768]{1,0:T(8,128)(2,1)}, bf16[48,3072]{1,0:T(8,128)(2,1)}, bf16[192,768]{1,0:T(8,128)(2,1)}), (bf16[48,2304]{1,0:T(8,128)(2,1)}, bf16[48,768]{1,0:T(8,128)(2,1)}, ...) | async-done | bytes 884752 | tf_op jit(solution)/shard_map/psum | solution.py:227
  1170.4 6.5 stack.81
  1177.0 4.7 multiply_add_fusion
  1181.6 42.1 %psum.47 = f32[10]{0:T(128)S(1)} all-reduce(f32[10]{0:T(128)S(1)} %stack.81), channel_id=1, replica_groups=mesh['dp'=2,'fsdp'=16] {'fsdp'}, use_global_device_ids=true, to_apply=%region_40.41 | all-reduce | flops 10 | bytes 80 | tf_op jit(solution)/shard_map/psum | solution.py:239
  (273 shorter events, 146.5 us)
Async XLA Ops:
  7.2 81.6 %all-gather.6.cloned.1.call-start = ((), (), s32[]{:S(2)}) async-start(), calls=%async_computation.5 | async-start | bytes 3760128 | tf_op jit(solution)/shard_map/all_gather | solution.py:94
  9.8 52.8 %copy-start.61 = (s32[2,392]{1,0:T(2,128)S(1)}, s32[2,392]{1,0:T(2,128)}, u32[]{:S(2)}) copy-start(s32[2,392]{1,0:T(2,128)} %param.20) | copy-start | bytes 9412
  9.8 52.9 %copy-start.18 = (bf16[2,392,768]{2,1,0:T(8,128)(2,1)S(1)}, bf16[2,392,768]{2,1,0:T(8,128)(2,1)}, u32[]{:S(2)}) copy-start(bf16[2,392,768]{2,1,0:T(8,128)(2,1)} %param.19) | copy-start | bytes 3612676
  9.8 142.9 %all-gather.8.cloned.1.call-start = ((), (), s32[]{:S(2)}) async-start(), calls=%async_computation.6 | async-start | bytes 1253376 | tf_op jit(solution)/shard_map/all_gather | solution.py:95
  12.2 214.2 %all-gather.10.cloned.1.call-start = ((), (), s32[]{:S(2)}) async-start(), calls=%async_computation.7 | async-start | bytes 5013504 | tf_op jit(solution)/shard_map/all_gather | solution.py:96
  15.0 293.8 %all-gather.12.cloned.1.call-start = ((), (), s32[]{:S(2)}) async-start(), calls=%async_computation.8 | async-start | bytes 5013504 | tf_op jit(solution)/shard_map/all_gather | solution.py:146
  18.3 650.8 %reduce-scatter.10.cloned.1.call-start = ((), (), s32[]{:S(2)}) async-start(), calls=%async_computation.10 | async-start | bytes 2506752 | tf_op jit(solution)/shard_map/reduce_scatter | solution.py:221
  329.4 341.2 %reduce-scatter.8.cloned.1.call-start = ((), (), s32[]{:S(2)}) async-start(), calls=%async_computation.9 | async-start | bytes 7520256 | tf_op jit(solution)/shard_map/reduce_scatter | solution.py:220
  427.8 412.0 %reduce-scatter.12.cloned.1.call-start = ((), (), s32[]{:S(2)}) async-start(), calls=%async_computation.11 | async-start | bytes 10027008 | tf_op jit(solution)/shard_map/reduce_scatter | solution.py:222
  438.2 577.2 %reduce-scatter.14.cloned.1.call-start = ((), (), s32[]{:S(2)}) async-start(), calls=%async_computation.12 | async-start | bytes 10027008 | tf_op jit(solution)/shard_map/reduce_scatter | solution.py:223
  447.7 124.5 %copy-start.51 = (f32[2,392]{1,0:T(2,128)S(1)}, f32[2,392]{1,0:T(2,128)}, u32[]{:S(2)}) copy-start(f32[2,392]{1,0:T(2,128)} %copy-done.50) | copy-start | bytes 9412
  447.7 136.6 %copy-start.11 = (f32[192,768]{1,0:T(8,128)S(1)}, f32[192,768]{1,0:T(8,128)}, u32[]{:S(2)}) copy-start(f32[192,768]{1,0:T(8,128)} %param.26) | copy-start | bytes 1769476
  447.8 693.9 %reduce-scatter.16.cloned.1.call-start = ((), (), s32[]{:S(2)}) async-start(), calls=%async_computation.13 | async-start | bytes 417792
  448.7 12.7 %collective-permute-start = (bf16[192,768]{1,0:T(8,128)(2,1)S(1)}, bf16[192,768]{1,0:T(8,128)(2,1)S(1)}, u32[]{:S(2)}, u32[]{:S(2)}) collective-permute-start(bf16[192,768]{1,0:T(8,128)(2,1)S(1)} %copy-done.21), channel_id=1, source_target_pairs={{0,1},{1,2},{2,3},{3,4},{4,5},{5,6},{6,7},{7,8},{8,9},{9,10},{10,1... | collective-permute-start | bytes 884744 | tf_op jit(solution)/shard_map/ppermute | solution.py:24
  462.1 11.1 collective-permute-start.1
  473.2 77.2 %copy-start.34 = (bf16[192,768]{1,0:T(8,128)(2,1)}, bf16[192,768]{1,0:T(8,128)(2,1)S(1)}, u32[]{:S(2)}) copy-start(bf16[192,768]{1,0:T(8,128)(2,1)S(1)} %collective-permute-done.1) | copy-start | bytes 884740
  473.2 18.5 %collective-permute-start.2 = (bf16[192,768]{1,0:T(8,128)(2,1)S(1)}, bf16[192,768]{1,0:T(8,128)(2,1)S(1)}, u32[]{:S(2)}, u32[]{:S(2)}) collective-permute-start(bf16[192,768]{1,0:T(8,128)(2,1)S(1)} %collective-permute-done.1), channel_id=1, source_target_pairs={{0,1},{1,2},{2,3},{3,4},{4,5},{5,6},{6,7},{7,8},{8,9},{9,10},{10,1... | collective-permute-start | bytes 884744 | tf_op jit(solution)/shard_map/ppermute | solution.py:24
  491.7 18.3 %collective-permute-start.3 = (bf16[192,768]{1,0:T(8,128)(2,1)S(1)}, bf16[192,768]{1,0:T(8,128)(2,1)S(1)}, u32[]{:S(2)}, u32[]{:S(2)}) collective-permute-start(bf16[192,768]{1,0:T(8,128)(2,1)S(1)} %collective-permute-done.2), channel_id=1, source_target_pairs={{0,1},{1,2},{2,3},{3,4},{4,5},{5,6},{6,7},{7,8},{8,9},{9,10},{10,1... | collective-permute-start | bytes 884744 | tf_op jit(solution)/shard_map/ppermute | solution.py:24
  510.1 17.5 %collective-permute-start.4 = (bf16[192,768]{1,0:T(8,128)(2,1)S(1)}, bf16[192,768]{1,0:T(8,128)(2,1)S(1)}, u32[]{:S(2)}, u32[]{:S(2)}) collective-permute-start(bf16[192,768]{1,0:T(8,128)(2,1)S(1)} %collective-permute-done.3), channel_id=1, source_target_pairs={{0,1},{1,2},{2,3},{3,4},{4,5},{5,6},{6,7},{7,8},{8,9},{9,10},{10,1... | collective-permute-start | bytes 884744 | tf_op jit(solution)/shard_map/ppermute | solution.py:24
  527.6 11.6 collective-permute-start.5
  539.9 10.5 collective-permute-start.6
  550.4 10.5 collective-permute-start.7
  560.9 10.6 collective-permute-start.8
  572.2 12.1 collective-permute-start.9
  584.4 13.5 %collective-permute-start.10 = (bf16[192,768]{1,0:T(8,128)(2,1)}, bf16[192,768]{1,0:T(8,128)(2,1)}, u32[]{:S(2)}, u32[]{:S(2)}) collective-permute-start(bf16[192,768]{1,0:T(8,128)(2,1)} %collective-permute-done.9), channel_id=1, source_target_pairs={{0,1},{1,2},{2,3},{3,4},{4,5},{5,6},{6,7},{7,8},{8,9},{9,10},{10,1... | collective-permute-start | bytes 884744 | tf_op jit(solution)/shard_map/ppermute | solution.py:24
  585.1 29.1 %copy-start.40 = (bf16[192,768]{1,0:T(8,128)(2,1)S(1)}, bf16[192,768]{1,0:T(8,128)(2,1)}, u32[]{:S(2)}) copy-start(bf16[192,768]{1,0:T(8,128)(2,1)} %copy-done.39) | copy-start | bytes 884740
  585.1 44.8 %copy-start.36 = (bf16[192,768]{1,0:T(8,128)(2,1)S(1)}, bf16[192,768]{1,0:T(8,128)(2,1)}, u32[]{:S(2)}) copy-start(bf16[192,768]{1,0:T(8,128)(2,1)} %copy-done.35) | copy-start | bytes 884740
  597.8 12.9 %collective-permute-start.11 = (bf16[192,768]{1,0:T(8,128)(2,1)}, bf16[192,768]{1,0:T(8,128)(2,1)S(1)}, u32[]{:S(2)}, u32[]{:S(2)}) collective-permute-start(bf16[192,768]{1,0:T(8,128)(2,1)} %collective-permute-done.10), channel_id=1, source_target_pairs={{0,1},{1,2},{2,3},{3,4},{4,5},{5,6},{6,7},{7,8},{8,9},{9,10},{10,1... | collective-permute-start | bytes 884744 | tf_op jit(solution)/shard_map/ppermute | solution.py:24
  610.8 19.2 %collective-permute-start.12 = (bf16[192,768]{1,0:T(8,128)(2,1)S(1)}, bf16[192,768]{1,0:T(8,128)(2,1)S(1)}, u32[]{:S(2)}, u32[]{:S(2)}) collective-permute-start(bf16[192,768]{1,0:T(8,128)(2,1)S(1)} %collective-permute-done.11), channel_id=1, source_target_pairs={{0,1},{1,2},{2,3},{3,4},{4,5},{5,6},{6,7},{7,8},{8,9},{9,10},{10,1... | collective-permute-start | bytes 884744 | tf_op jit(solution)/shard_map/ppermute | solution.py:24
  630.0 12.2 collective-permute-start.13
  642.2 12.2 collective-permute-start.14
  668.0 349.2 %copy-start.58 = (f32[768]{0:T(1024)S(1)}, f32[768]{0:T(1024)}, u32[]{:S(2)}) copy-start(f32[768]{0:T(1024)} %get-tuple-element.62) | copy-start | bytes 9220
  669.0 494.8 %all-reduce.3.cloned.1.call-start = ((), (), s32[]{:S(2)}) async-start(), calls=%async_computation.14 | async-start | bytes 1769472 | tf_op jit(solution)/shard_map/psum | solution.py:227
  1017.2 159.6 %copy-start.47 = (f32[784]{0:T(1024)S(1)}, f32[784]{0:T(1024)}, u32[]{:S(2)}) copy-start(f32[784]{0:T(1024)} %copy-done.46) | copy-start | bytes 9412
  1017.2 159.6 %copy-start.49 = (f32[784]{0:T(1024)S(1)}, f32[784]{0:T(1024)}, u32[]{:S(2)}) copy-start(f32[784]{0:T(1024)} %copy-done.48) | copy-start | bytes 9412
  1176.8 57.6 %copy-start.53 = (f32[48,12]{0,1:T(8,128)S(1)}, f32[48,12]{0,1:T(8,128)}, u32[]{:S(2)}) copy-start(f32[48,12]{0,1:T(8,128)} %param.27) | copy-start | bytes 6916
  1176.8 57.6 %copy-start.56 = (f32[48,12]{0,1:T(8,128)S(1)}, f32[48,12]{0,1:T(8,128)}, u32[]{:S(2)}) copy-start(f32[48,12]{0,1:T(8,128)} %param.37) | copy-start | bytes 6916
  1176.9 57.6 %copy-start.57 = (f32[48,12]{0,1:T(8,128)S(1)}, f32[48,12]{0,1:T(8,128)}, u32[]{:S(2)}) copy-start(f32[48,12]{0,1:T(8,128)} %param.32) | copy-start | bytes 6916
  1176.9 58.2 %copy-start.23 = (f32[48,768]{1,0:T(8,128)S(1)}, f32[48,768]{1,0:T(8,128)}, u32[]{:S(2)}) copy-start(f32[48,768]{1,0:T(8,128)} %param.24) | copy-start | bytes 442372
  1176.9 58.2 %copy-start.30 = (bf16[48,768]{1,0:T(8,128)(2,1)S(1)}, bf16[48,768]{1,0:T(8,128)(2,1)}, u32[]{:S(2)}) copy-start(bf16[48,768]{1,0:T(8,128)(2,1)} %get-tuple-element.71) | copy-start | bytes 221188
  1176.9 58.2 %copy-start.41 = (f32[48,768]{1,0:T(8,128)S(1)}, f32[48,768]{1,0:T(8,128)}, u32[]{:S(2)}) copy-start(f32[48,768]{1,0:T(8,128)} %param.34) | copy-start | bytes 442372
  1176.9 58.2 %copy-start.42 = (f32[48,768]{1,0:T(8,128)S(1)}, f32[48,768]{1,0:T(8,128)}, u32[]{:S(2)}) copy-start(f32[48,768]{1,0:T(8,128)} %param.29) | copy-start | bytes 442372
  1176.9 59.0 %copy-start.16 = (f32[48,2304]{1,0:T(8,128)S(1)}, f32[48,2304]{1,0:T(8,128)}, u32[]{:S(2)}) copy-start(f32[48,2304]{1,0:T(8,128)} %param.23) | copy-start | bytes 1327108
  1176.9 59.0 %copy-start.22 = (bf16[48,2304]{1,0:T(8,128)(2,1)S(1)}, bf16[48,2304]{1,0:T(8,128)(2,1)}, u32[]{:S(2)}) copy-start(bf16[48,2304]{1,0:T(8,128)(2,1)} %get-tuple-element.70) | copy-start | bytes 663556
  1176.9 59.0 %copy-start.29 = (f32[48,2304]{1,0:T(8,128)S(1)}, f32[48,2304]{1,0:T(8,128)}, u32[]{:S(2)}) copy-start(f32[48,2304]{1,0:T(8,128)} %param.33) | copy-start | bytes 1327108
  1181.6 56.5 %copy-start.20 = (bf16[192,768]{1,0:T(8,128)(2,1)S(1)}, bf16[192,768]{1,0:T(8,128)(2,1)}, u32[]{:S(2)}) copy-start(bf16[192,768]{1,0:T(8,128)(2,1)} %get-tuple-element.73) | copy-start | bytes 884740
  1181.6 57.9 %copy-start.15 = (f32[48,3072]{1,0:T(8,128)S(1)}, f32[48,3072]{1,0:T(8,128)}, u32[]{:S(2)}) copy-start(f32[48,3072]{1,0:T(8,128)} %param.25) | copy-start | bytes 1769476
  1181.6 57.9 %copy-start.19 = (bf16[48,3072]{1,0:T(8,128)(2,1)S(1)}, bf16[48,3072]{1,0:T(8,128)(2,1)}, u32[]{:S(2)}) copy-start(bf16[48,3072]{1,0:T(8,128)(2,1)} %get-tuple-element.72) | copy-start | bytes 884740
  (41 other events, 344.7 us)
Sparse Core Ops, SparseCore 0:
  11.4 74.1 all-gather.5
  89.0 54.6 all-gather.7
  147.1 79.3 all-gather.9
  229.7 79.0 all-gather.11
  329.6 127.0 reduce-scatter.9
  462.7 200.2 reduce-scatter.7
  669.7 170.1 reduce-scatter.11
  845.5 169.7 reduce-scatter.13
  1021.3 120.3 reduce-scatter.15
  1145.2 18.4 all-reduce.2
